TPU v7x, 32 devices: a whole 2x2x4 slice. The times are simulated.
32 devices in a mesh: groups: 2 (over y), seq: 8 (over z, x), head: 2 (over core).
Axes of the slice: x: 2, y: 2, z: 4, core: 2. Of those that a mesh axis runs over, the one named last changes fastest.
Arguments:
- mixer_input: bfloat16 [2048, 8192], P(('groups', 'seq'), 'head'), parts along dimension 0, may hold values from -6 to 6
- keys_queries: bfloat16 [2048, 2, 512], P(('groups', 'seq'), None, 'head'), parts along dimension 0, may hold values from -6 to 6
- gate_input: bfloat16 [2048, 8192], P(('groups', 'seq'), 'head'), parts along dimension 0, may hold values from -6 to 6
- step_raw: bfloat16 [2048, 128], P(('groups', 'seq'), 'head'), parts along dimension 0, may hold values from -4 to 4
- mixer_weight: bfloat16 [4, 8192], P(None, 'head'), may hold values from -3 to 3
- mixer_bias: bfloat16 [8192], P('head'), may hold values from -3 to 3
- keyquery_weight: bfloat16 [4, 2, 512], P(None, None, 'head'), may hold values from -3 to 3
- keyquery_bias: bfloat16 [2, 512], P(None, 'head'), may hold values from -3 to 3
- step_bias: float32 [128], P('head'), may hold values from -4 to -1
- decay_log: float32 [128], P('head'), may hold values from -14 to 0
- skip_gain: float32 [128], P('head'), may hold values from 0.5 to 2
- norm_gain: float32 [8192], P('head'), may hold values from 0.25 to 1.75
- resets: int32 [16], P(('groups', 'seq')), parts along dimension 0, may hold values from 0 to 1, as said below
Outputs:
- mixed: bfloat16 [2048, 8192], P(('groups', 'seq'), 'head'), parts along dimension 0
There are 2 independent parts, one for each index of `groups`. A program takes and returns all parts, laid end to end along the dimension named above; an argument that names none is the same for every part. Nothing has to cross between parts.
Inputs may be any that keep to these rules, and one draw needn't show every extreme that they name: resets[c] = 1 marks a document that starts at the first token of span c; some span after the first holds a 1.
All inputs are finite; a program needn't handle non-finite values.
Results may differ from a plain program's by a relative error of at most 0.0044.
The roundings to bfloat16 on the way count: a program that leaves them out, or rounds other values in their place, can miss the bound.
Values may be sent and summed in bfloat16 or wider, within the bound.
A program may use at most 64 MiB of HBM per device.

v0:
```python
import jax
import jax.numpy as jnp
from jax import lax
from jax.sharding import PartitionSpec as P

HEAD_DEV = 64
GRP_DEV = 2
HEAD_SIZE = 64
STATE = 128
SPAN = 128
KERNEL = 4


def shifted_2(shard, axis, by):
    peers = lax.axis_size(axis)
    pairs = [(i, i + by) for i in range(peers) if 0 <= i + by < peers]
    return lax.ppermute(shard, axis, pairs)


def convolve(rim_block, raw_rows, weight, bias_row, survive):
    length, channels = raw_rows.shape
    rim_count = KERNEL - 1
    blocks = length // SPAN
    raw_blocks = raw_rows.reshape(blocks, SPAN, channels)
    prior = jnp.concatenate([rim_block[None], raw_blocks[:-1, SPAN - rim_count :]], axis=0)
    prior = prior * survive[:, None, None].astype(jnp.bfloat16)
    extended = jnp.concatenate([prior, raw_blocks], axis=1)
    running = lax.conv_general_dilated(
        extended,
        weight[:, None, :],
        (1,),
        "VALID",
        dimension_numbers=("NWC", "WIO", "NWC"),
        feature_group_count=channels,
        preferred_element_type=jnp.float32,
    )
    running = running + bias_row.astype(jnp.float32)
    return jax.nn.silu(running).astype(jnp.bfloat16).reshape(length, channels)


def compose(earlier, latter):
    return (earlier[0] * latter[0], latter[0] * earlier[1] + latter[1])


def route_state(factor, local_state):
    devices = lax.axis_size("seq")
    piece_width = local_state.size // devices
    arrived = lax.all_to_all(
        local_state.reshape(devices, piece_width), "seq", split_axis=0, concat_axis=0, tiled=True
    )
    gathered = lax.all_gather(factor[None, :], "seq", axis=0, tiled=True)
    offset = lax.axis_index("seq") * piece_width
    head_of = (offset + jnp.arange(piece_width, dtype=jnp.int32)) // (HEAD_SIZE * STATE)
    selector = (jnp.arange(HEAD_DEV, dtype=jnp.int32)[:, None] == head_of[None, :]).astype(
        jnp.float32
    )
    spread = jnp.dot(gathered, selector, precision=lax.Precision.HIGHEST)
    _, through = lax.associative_scan(compose, (spread, arrived), axis=0)
    shifted = jnp.concatenate([jnp.zeros((1, piece_width), jnp.float32), through[:-1]], axis=0)
    returned = lax.all_to_all(shifted, "seq", split_axis=0, concat_axis=0, tiled=True)
    incoming = returned.reshape(local_state.shape)
    return incoming


def shards(
    mixer_input,
    keys_queries,
    gate_input,
    step_raw,
    mixer_weight,
    mixer_bias,
    keyquery_weight,
    keyquery_bias,
    step_bias,
    decay_log,
    skip_gain,
    norm_gain,
    resets,
):
    length, features = mixer_input.shape
    rim_count = KERNEL - 1
    blocks = length // SPAN
    heads_group = HEAD_DEV // GRP_DEV
    pair_flat = keys_queries.reshape(length, -1)
    pair_width = pair_flat.shape[1]
    half_width = pair_width // 2
    edge_rows = jnp.concatenate(
        [mixer_input[length - rim_count :], pair_flat[length - rim_count :]], axis=1
    )
    arrived = shifted_2(edge_rows, "seq", 1)
    rim_mixer = arrived[:, :features]
    rim_pair = arrived[:, features:]
    survive = 1.0 - resets.astype(jnp.float32)
    value_conv = convolve(rim_mixer, mixer_input, mixer_weight, mixer_bias, survive)
    pair_conv = convolve(
        rim_pair,
        pair_flat,
        keyquery_weight.reshape(KERNEL, pair_width),
        keyquery_bias.reshape(pair_width),
        survive,
    )
    value_rows = value_conv.reshape(blocks, SPAN, HEAD_DEV, HEAD_SIZE)
    key_rows = pair_conv[:, :half_width].reshape(blocks, SPAN, GRP_DEV, STATE)
    query_rows = pair_conv[:, half_width:].reshape(blocks, SPAN, GRP_DEV, STATE)
    step_size = jax.nn.softplus(step_raw.astype(jnp.float32) + step_bias).reshape(
        blocks, SPAN, HEAD_DEV
    )
    cumulative = jnp.cumsum(-jnp.exp(decay_log) * step_size, axis=1)
    scores = jnp.einsum("cqgn,cugn->cgqu", query_rows, key_rows, preferred_element_type=jnp.float32)
    head_cum = jnp.swapaxes(cumulative, 1, 2)
    log_gaps = head_cum[:, :, :, None] - head_cum[:, :, None, :]
    causal = jnp.arange(SPAN)[:, None] >= jnp.arange(SPAN)[None, :]
    decays = jnp.exp(jnp.where(causal, log_gaps, -jnp.inf)).reshape(
        blocks, GRP_DEV, heads_group, SPAN, SPAN
    )
    step_cols = jnp.swapaxes(step_size, 1, 2).reshape(blocks, GRP_DEV, heads_group, 1, SPAN)
    mixing = (
        (scores[:, :, None] * decays * step_cols)
        .astype(jnp.bfloat16)
        .reshape(blocks, HEAD_DEV, SPAN, SPAN)
    )
    inside = jnp.einsum("chqu,cuhp->cqhp", mixing, value_rows, preferred_element_type=jnp.float32)
    span_end = cumulative[:, -1]
    weighted = (
        jnp.exp(span_end[:, None, :] - cumulative)[..., None]
        * step_size[..., None]
        * value_rows.astype(jnp.float32)
    ).astype(jnp.bfloat16)
    states = jnp.einsum(
        "cugkp,cugn->cgkpn",
        weighted.reshape(blocks, SPAN, GRP_DEV, heads_group, HEAD_SIZE),
        key_rows,
        preferred_element_type=jnp.float32,
    ).reshape(blocks, HEAD_DEV, HEAD_SIZE, STATE)
    span_decay = jnp.exp(span_end)
    local_state = jnp.zeros((HEAD_DEV, HEAD_SIZE, STATE), jnp.float32)
    factor = jnp.ones((HEAD_DEV,), jnp.float32)
    held_state = survive[0] * local_state
    scale_in = survive[0] * factor
    held_list = [held_state]
    factor_list = [scale_in]
    local_state = span_decay[0][:, None, None] * held_state + states[0]
    factor = span_decay[0] * scale_in
    held_all = jnp.stack(held_list)
    factor_all = jnp.stack(factor_list)
    queries_float = query_rows.astype(jnp.float32)
    growth = jnp.exp(cumulative)[..., None]
    skip_term = skip_gain[:, None] * value_rows.astype(jnp.float32)
    incoming = route_state(factor, local_state)
    entering = held_all + factor_all[:, :, None, None] * incoming[None]
    read_back = jnp.einsum(
        "cqgn,cgkpn->cqgkp",
        queries_float,
        entering.reshape(blocks, GRP_DEV, heads_group, HEAD_SIZE, STATE),
        precision=lax.Precision.HIGHEST,
    ).reshape(blocks, SPAN, HEAD_DEV, HEAD_SIZE)
    result = inside + growth * read_back + skip_term
    gated = result.reshape(length, features) * jax.nn.silu(gate_input.astype(jnp.float32))
    grouped = gated.reshape(length, GRP_DEV, -1)
    mean_square = jnp.mean(grouped * grouped, axis=-1, keepdims=True)
    normed = (grouped * lax.rsqrt(mean_square + 1e-05)).reshape(length, features) * norm_gain
    return normed.astype(jnp.bfloat16)


def solution(mesh):
    in_specs = (
        P(("groups", "seq"), "head"),
        P(("groups", "seq"), None, "head"),
        P(("groups", "seq"), "head"),
        P(("groups", "seq"), "head"),
        P(None, "head"),
        P("head"),
        P(None, None, "head"),
        P(None, "head"),
        P("head"),
        P("head"),
        P("head"),
        P("head"),
        P(("groups", "seq")),
    )
    out_specs = P(("groups", "seq"), "head")
    return jax.shard_map(shards, mesh=mesh, in_specs=in_specs, out_specs=out_specs, check_vma=False)
```

profile of v0, /device:TPU:0, one launch (start us, length us, event | category | flops | bytes accessed | tf_op | source)
XLA Modules:
  0.0 317.9 jit_solution(17780342998690467485)
XLA Ops:
  1.6 4.8 %collective-permute-start = (bf16[3,4608]{1,0:T(4,128)(2,1)S(1)}, bf16[3,4608]{1,0:T(4,128)(2,1)S(1)}, u32[]{:S(2)}, u32[]{:S(2)}) collective-permute-start(bf16[3,4608]{1,0:T(4,128)(2,1)S(1)} %pad_maximum_fusion.2), channel_id=1, source_target_pairs={{0,2},{2,4},{4,6},{6,8},{8,10},{10,12},{12,14},{1,3},{3,5},{5,7},{... | collective-permute-start | bytes 82952 | tf_op jit(solution)/shard_map/ppermute | solution.py:17
  23.8 3.5 %add.140 = f32[8,1,65536]{2,1,0:T(1,128)} add(f32[8,1,65536]{2,1,0:T(1,128)S(1)} %bitcast.111, f32[8,1,65536]{2,1,0:T(1,128)S(1)} %bitcast.110) | non-fusion elementwise | flops 524288 | bytes 6291456 | tf_op jit(solution)/shard_map/add | solution.py:142
  27.3 4.9 %all-to-all-start = ((f32[8,1,65536]{2,1,0:T(1,128)}), f32[8,1,65536]{2,1,0:T(1,128)}, u32[]{:S(2)}, u32[]{:S(2)}) async-start(f32[8,1,65536]{2,1,0:T(1,128)} %add.140), calls=%async_computation | async-start | bytes 4194304 | tf_op jit(solution)/shard_map/all_to_all | solution.py:48
  32.1 48.9 %all-gather = f32[8,1,64]{2,1,0:T(1,128)S(1)} all-gather(f32[1,1,64]{2,1,0:T(1,128)S(1)} %get-tuple-element.17), channel_id=2, replica_groups=mesh['groups'=2,'seq'=8,'head'=2] {'seq'}, dimensions={0}, use_global_device_ids=true | all-gather | bytes 2304 | tf_op jit(solution)/shard_map/all_gather | solution.py:51
  81.2 6.5 %fusion = f32[8,65536]{1,0:T(8,128)} fusion(f32[8,64]{1,0:T(8,128)S(1)} %bitcast.124, s32[65536]{0:T(1024)S(1)} %add_select_fusion), kind=kOutput, calls=%fused_computation.1 | convolution fusion | flops 406847488 | bytes 2361344 | tf_op jit(solution)/shard_map/dot_general | solution.py:57
  87.8 10.7 %slice.103 = f32[3,65536]{1,0:T(4,128)} slice(f32[8,65536]{1,0:T(8,128)} %fusion), slice={[2:8:2], [0:65536:1]} | slice | bytes 1572864 | tf_op jit(solution)/shard_map/slice | solution.py:58
  98.5 10.7 %slice.108 = f32[4,65536]{1,0:T(4,128)} slice(f32[8,65536]{1,0:T(8,128)} %fusion), slice={[0:7:2], [0:65536:1]} | slice | bytes 2097152 | tf_op jit(solution)/shard_map/slice | solution.py:58
  109.2 10.7 %slice.104 = f32[4,65536]{1,0:T(4,128)} slice(f32[8,65536]{1,0:T(8,128)} %fusion), slice={[1:8:2], [0:65536:1]} | slice | bytes 2097152 | tf_op jit(solution)/shard_map/slice | solution.py:58
  119.8 4.1 %copy.168 = f32[8,1,65536]{2,0,1:T(8,128)} copy(f32[8,1,65536]{2,1,0:T(1,128)} %all-to-all-done) | data formatting | bytes 4194304
  124.0 10.7 %slice.120 = f32[3,65536]{1,0:T(4,128)} slice(f32[8,65536]{1,0:T(8,128)} %bitcast.106), slice={[2:8:2], [0:65536:1]} | slice | bytes 1572864 | tf_op jit(solution)/shard_map/slice | solution.py:58
  134.6 10.7 %slice.106 = f32[4,65536]{1,0:T(4,128)} slice(f32[8,65536]{1,0:T(8,128)} %bitcast.107), slice={[1:8:2], [0:65536:1]} | slice | bytes 2097152 | tf_op jit(solution)/shard_map/slice | solution.py:58
  145.3 10.7 %slice.105 = f32[4,65536]{1,0:T(4,128)} slice(f32[8,65536]{1,0:T(8,128)} %bitcast.108), slice={[0:7:2], [0:65536:1]} | slice | bytes 2097152 | tf_op jit(solution)/shard_map/slice | solution.py:58
  156.0 3.8 %fusion.58 = (f32[4,65536]{1,0:T(4,128)}, f32[4,65536]{1,0:T(4,128)S(1)}) fusion(f32[4,65536]{1,0:T(4,128)} %slice.108, f32[4,65536]{1,0:T(4,128)} %slice.104, f32[4,65536]{1,0:T(4,128)} %slice.106, f32[4,65536]{1,0:T(4,128)} %slice.105), kind=kLoop, calls=%fused_computation.109 | loop fusion | flops 786432 | bytes 6291456 | tf_op jit(solution)/shard_map/mul | solution.py:42
  159.8 7.0 %slice.112 = f32[2,65536]{1,0:T(2,128)} slice(f32[4,65536]{1,0:T(4,128)S(1)} %get-tuple-element.10), slice={[1:4:2], [0:65536:1]} | slice | bytes 1048576 | tf_op jit(solution)/shard_map/slice | solution.py:58
  166.7 6.9 %slice.111 = f32[2,65536]{1,0:T(2,128)} slice(f32[4,65536]{1,0:T(4,128)S(1)} %get-tuple-element.10), slice={[0:3:2], [0:65536:1]} | slice | bytes 1048576 | tf_op jit(solution)/shard_map/slice | solution.py:58
  173.7 10.1 %slice.110 = f32[2,65536]{1,0:T(2,128)} slice(f32[4,65536]{1,0:T(4,128)} %get-tuple-element.9), slice={[1:4:2], [0:65536:1]} | slice | bytes 1048576 | tf_op jit(solution)/shard_map/slice | solution.py:58
  183.8 10.1 %slice.114 = f32[2,65536]{1,0:T(2,128)} slice(f32[4,65536]{1,0:T(4,128)} %get-tuple-element.9), slice={[0:3:2], [0:65536:1]} | slice | bytes 1048576 | tf_op jit(solution)/shard_map/slice | solution.py:58
  197.7 2.8 fusion.57
  200.5 4.4 %pad.23 = f32[4,65536]{1,0:T(4,128)S(1)} pad(f32[2,65536]{1,0:T(2,128)} %pad_add_fusion, f32[]{:T(128)} %constant.41.clone.1), padding=1_0_1x0_0_0 | pad | bytes 1572868 | tf_op jit(solution)/shard_map/pad | solution.py:58
  204.9 2.2 pad_maximum_fusion.1
  207.1 8.1 %pad.22 = f32[4,65536]{1,0:T(4,128)} pad(f32[2,65536]{1,0:T(2,128)} %pad_maximum_fusion.1, f32[]{:T(128)} %constant.41.clone.1), padding=0_1_1x0_0_0 | pad | bytes 1572868 | tf_op jit(solution)/shard_map/pad | solution.py:58
  215.3 2.6 add.148
  220.8 8.9 %pad.51 = f32[7,65536]{1,0:T(8,128)} pad(f32[4,65536]{1,0:T(4,128)} %pad_maximum_fusion, f32[]{:T(128)} %constant.41.clone.1), padding=0_0_1x0_0_0 | pad | bytes 2883588 | tf_op jit(solution)/shard_map/slice | solution.py:59
  229.7 5.0 %pad.93 = f32[8,65536]{1,0:T(8,128)} pad(f32[4,65536]{1,0:T(4,128)S(1)} %copy-done.6, f32[]{:T(128)} %constant.41.clone.1), padding=1_0_1x0_0_0 | pad | bytes 3145732
  234.6 2.4 slice_add_fusion.2
  237.4 3.5 %copy.146 = f32[8,1,65536]{2,1,0:T(1,128)} copy(f32[8,1,65536]{2,0,1:T(8,128)S(1)} %pad_bitcast_fusion) | data formatting | bytes 4194304 | tf_op jit(solution)/shard_map/all_to_all | solution.py:60
  240.8 10.8 %all-to-all-start.1 = ((f32[8,1,65536]{2,1,0:T(1,128)}), f32[8,1,65536]{2,1,0:T(1,128)}, u32[]{:S(2)}, u32[]{:S(2)}) async-start(f32[8,1,65536]{2,1,0:T(1,128)} %copy.146), calls=%async_computation.1 | async-start | bytes 4194304 | tf_op jit(solution)/shard_map/all_to_all | solution.py:60
  253.9 2.3 fusion.4
  256.2 41.3 %all-to-all-done.1 = f32[8,1,65536]{2,1,0:T(1,128)} async-done(((f32[8,1,65536]{2,1,0:T(1,128)}), f32[8,1,65536]{2,1,0:T(1,128)}, u32[]{:S(2)}, u32[]{:S(2)}) %all-to-all-start.1) | async-done | bytes 2097184 | tf_op jit(solution)/shard_map/all_to_all | solution.py:60
  300.8 3.0 fusion.13
  307.7 4.0 %mul.271 = f32[128,2,2048]{2,1,0:T(2,128)} reshape(f32[128,4096]{1,0:T(8,128)} %fusion.55) | data formatting | bytes 4194304 | tf_op jit(solution)/shard_map/mul | solution.py:160
  311.7 2.2 reduce_sum.9
  (103 shorter events, 38.6 us)
Async XLA Ops:
  0.0 16.8 %copy-start = (bf16[4,4096]{1,0:T(4,128)(2,1)S(1)}, bf16[4,4096]{1,0:T(4,128)(2,1)}, u32[]{:S(2)}) copy-start(bf16[4,4096]{1,0:T(4,128)(2,1)} %param.17) | copy-start | bytes 98308
  0.0 14.3 %copy-start.18 = (pred[8,17]{0,1:T(8,128)(4,1)S(1)}, pred[8,17]{0,1:T(8,128)(4,1)}, u32[]{:S(2)}) copy-start(pred[8,17]{0,1:T(8,128)(4,1)} %constant.76) | copy-start | bytes 412
  1.6 12.4 %collective-permute-start = (bf16[3,4608]{1,0:T(4,128)(2,1)S(1)}, bf16[3,4608]{1,0:T(4,128)(2,1)S(1)}, u32[]{:S(2)}, u32[]{:S(2)}) collective-permute-start(bf16[3,4608]{1,0:T(4,128)(2,1)S(1)} %pad_maximum_fusion.2), channel_id=1, source_target_pairs={{0,2},{2,4},{4,6},{6,8},{8,10},{10,12},{12,14},{1,3},{3,5},{5,7},{... | collective-permute-start | bytes 82952 | tf_op jit(solution)/shard_map/ppermute | solution.py:17
  14.2 1.2 copy-start.10
  15.3 7.8 %copy-start.11 = (bf16[128,256]{0,1:T(8,128)(2,1)}, bf16[128,256]{0,1:T(8,128)(2,1)S(1)}, u32[]{:S(2)}) copy-start(bf16[128,256]{0,1:T(8,128)(2,1)S(1)} %copy.134) | copy-start | bytes 196612
  27.3 92.6 %all-to-all-start = ((f32[8,1,65536]{2,1,0:T(1,128)}), f32[8,1,65536]{2,1,0:T(1,128)}, u32[]{:S(2)}, u32[]{:S(2)}) async-start(f32[8,1,65536]{2,1,0:T(1,128)} %add.140), calls=%async_computation | async-start | bytes 4194304 | tf_op jit(solution)/shard_map/all_to_all | solution.py:48
  193.9 1.8 copy-start.8
  193.9 1.8 copy-start.9
  215.2 2.6 copy-start.2
  215.2 2.6 copy-start.4
  215.3 2.6 copy-start.5
  220.8 8.9 %copy-start.6 = (f32[4,65536]{1,0:T(4,128)S(1)}, f32[4,65536]{1,0:T(4,128)}, u32[]{:S(2)}) copy-start(f32[4,65536]{1,0:T(4,128)} %add.148) | copy-start | bytes 3145732
  240.8 10.8 %copy-start.14 = (f32[64,128]{0,1:T(8,128)S(1)}, f32[64,128]{0,1:T(8,128)}, u32[]{:S(2)}) copy-start(f32[64,128]{0,1:T(8,128)} %get-tuple-element.19) | copy-start | bytes 98308
  240.8 11.0 %copy-start.13 = (f32[128,64]{1,0:T(8,128)S(1)}, f32[128,64]{1,0:T(8,128)}, u32[]{:S(2)}) copy-start(f32[128,64]{1,0:T(8,128)} %get-tuple-element.15) | copy-start | bytes 98308
  240.8 11.1 %copy-start.15 = (bf16[128,256]{1,0:T(8,128)(2,1)S(1)}, bf16[128,256]{1,0:T(8,128)(2,1)}, u32[]{:S(2)}) copy-start(bf16[128,256]{1,0:T(8,128)(2,1)} %get-tuple-element.13) | copy-start | bytes 196612
  240.8 56.6 %all-to-all-start.1 = ((f32[8,1,65536]{2,1,0:T(1,128)}), f32[8,1,65536]{2,1,0:T(1,128)}, u32[]{:S(2)}, u32[]{:S(2)}) async-start(f32[8,1,65536]{2,1,0:T(1,128)} %copy.146), calls=%async_computation.1 | async-start | bytes 4194304 | tf_op jit(solution)/shard_map/all_to_all | solution.py:60
  251.6 2.0 copy-start.12
  299.2 1.6 copy-start.3
  299.2 1.6 copy-start.17
  303.8 2.0 copy-start.7
  314.5 1.7 copy-start.16
  316.2 1.7 copy-start.1
where the time goes:
time: 323 us; the launch traced here: 318 us
  local copies, waits for them, and re-layouts  154 us (48%)
  blocking collectives  48.9 us (15%)
  waiting for transfers between devices  41.3 us (13%)
  other arithmetic  39.8 us (12%)
  starting transfers between devices  20.5 us (6%)
  matrix products  12.7 us (4%)
    slice x11, local copies, waits for them, and re-layouts, route_state(): _, through = lax.associative_scan(compose, (spread, arrived), axis=0)  99.2 us
    all_gather x1, blocking collectives, route_state(): gathered = lax.all_gather(factor[None, :], 'seq', axis=0, tiled=True)  48.9 us
    all_to_all x1, waiting for transfers between devices, route_state(): lax.all_to_all(shifted, 'seq', split_axis=0, concat_axis=0, tiled=True)  41.3 us
    unnamed x45, local copies, waits for them, and re-layouts  12.9 us
    pad x2, local copies, waits for them, and re-layouts, route_state(): _, through = lax.associative_scan(compose, (spread, arrived), axis=0)  12.5 us
    all_to_all x1, starting transfers between devices, route_state(): lax.all_to_all(shifted, 'seq', split_axis=0, concat_axis=0, tiled=True)  10.8 us
    slice x1, local copies, waits for them, and re-layouts, route_state(): through[:-1]  8.85 us
    dot_general x1, matrix products, route_state(): spread = jnp.dot(gathered, selector, precision=lax.Precision.HIGHEST)  6.52 us
  transfers between devices with their start and end apart: 3, of which 1 were waited for; matrix products, arithmetic and copies ran while one was open for 16% of the time, Pallas kernels for 0%

commit v1 on v0

v1 whole, which is shorter than its diff:
```python
import functools

import jax
import jax.numpy as jnp
from jax import lax
from jax.experimental import pallas as pl
from jax.experimental.pallas import tpu as pltpu
from jax.sharding import PartitionSpec as P

HEAD_DEV = 64
GRP_DEV = 2
HEAD_SIZE = 64
STATE = 128
SPAN = 128
KERNEL = 4
RIM = KERNEL - 1
TILE = 256
TILE_HEADS = TILE // HEAD_SIZE
LOG2E = 1.4426950408889634
F32 = jnp.float32
BF16 = jnp.bfloat16
MESH = pl.DeviceIdType.MESH


def silu(x):
    half = 0.5 * x
    return half * jnp.tanh(half) + half


def two_terms(x):
    lane = lax.broadcasted_iota(jnp.int32, x.shape, 1)
    lead = x.astype(BF16).astype(F32)
    return jnp.where(lane < HEAD_DEV, lead, x - lead).astype(BF16)


def dot(a, b):
    return jnp.dot(a, b, preferred_element_type=F32)


def kernel(
    peers, tiles, split,
    x_ref, kq_ref, gate_ref, step_ref, wx_ref, bx_ref, wkq_ref, bkq_ref,
    sbias_ref, dlog_ref, skip_ref, gain_ref, resets_ref,
    out_ref,
    halo_send, halo_recv, halo, xs, kqs, vals, hot, w2, g2, cum2, row_t, keys_t, queries, scores, mask,
    rows2, f_send, f_recv, s_send, s_recv, s_own, c_recv, c_send, e_send, e_recv, e_own, res, mix_gate, ssq,
    one_send, one_recv, s_ssem, s_rsem, c_ssem, c_rsem, e_ssem, e_rsem,
):
    me = lax.axis_index("seq")
    side = lax.rem(me, 2)
    row = me // 2
    partner = me + 1 - 2 * side
    last_row = peers // 2 - 1
    features = tiles * TILE
    half_tiles = tiles // 2
    quarter = split

    barrier = pltpu.get_barrier_semaphore()
    for away in (-2, -1, 1, 2):
        @pl.when((me + away >= 0) & (me + away < peers))
        def _(away=away):
            pl.semaphore_signal(barrier, inc=1, device_id={"seq": me + away}, device_id_type=MESH)
    rim = jnp.concatenate(
        [x_ref[SPAN - 16 :, :].astype(F32)[16 - RIM :], kq_ref[SPAN - 16 :, :].astype(F32)[16 - RIM :]], axis=1
    )
    rim_parts = [rim[:, q * quarter : (q + 1) * quarter] for q in range(4)]
    halo_send[...] = jnp.concatenate(rim_parts + [jnp.zeros((4, quarter), F32)], axis=0).astype(BF16)
    pl.semaphore_wait(barrier, jnp.minimum(me, 2) + jnp.minimum(peers - 1 - me, 2))

    def remote(src, dst, ssem, rsem, target):
        return pltpu.make_async_remote_copy(
            src_ref=src, dst_ref=dst, send_sem=ssem, recv_sem=rsem, device_id={"seq": target}, device_id_type=MESH
        )

    halo_copy = remote(halo_send, halo_recv, one_send.at[0], one_recv.at[0], jnp.minimum(me + 1, peers - 1))

    @pl.when(me < peers - 1)
    def _():
        halo_copy.start()

    @pl.when(me == 0)
    def _():
        halo_recv[...] = jnp.zeros_like(halo_recv)

    survive = 1.0 - resets_ref[0].astype(F32)

    raw = step_ref[...].astype(F32)
    both = jnp.concatenate([raw, raw], axis=1)
    sbias = sbias_ref[...]
    dlog = dlog_ref[...]
    skip = skip_ref[...]
    logit = both + jnp.concatenate([sbias, sbias], axis=1)
    step = jnp.maximum(logit, 0.0) + jnp.log1p(jnp.exp(-jnp.abs(logit)))
    rate = (-LOG2E * jnp.exp(jnp.concatenate([dlog, dlog], axis=1))) * step
    t_idx = lax.broadcasted_iota(jnp.int32, (SPAN, SPAN), 0)
    s_idx = lax.broadcasted_iota(jnp.int32, (SPAN, SPAN), 1)
    lower = (t_idx >= s_idx).astype(F32)
    cum = jnp.dot(lower, rate, precision=lax.Precision.HIGHEST, preferred_element_type=F32)
    cum2[...] = cum
    end = cum[SPAN - 1 :, :]
    w2[...] = two_terms(jnp.exp2(end - cum) * step)
    g2[...] = two_terms(jnp.exp2(cum) * survive)
    factor = jnp.exp2(end) * survive
    f_send[...] = jnp.broadcast_to(factor, f_send.shape)
    f_copy = remote(f_send, f_recv, one_send.at[1], one_recv.at[1], partner)
    f_copy.start()
    row_t[...] = jnp.transpose(cum - jnp.log2(step))
    mask[...] = jnp.where(t_idx >= s_idx, 0.0, -1e30)

    @pl.loop(0, tiles)
    def _(t):
        r = lax.broadcasted_iota(jnp.int32, (SPAN, TILE), 0)
        c = lax.broadcasted_iota(jnp.int32, (SPAN, TILE), 1)
        hot[:, pl.ds(pl.multiple_of(t * TILE, TILE), TILE)] = (
            ((r & (HEAD_DEV - 1)) == t * TILE_HEADS + (c >> 6)).astype(F32).astype(BF16)
        )

    @pl.when(row == 0)
    def _():
        @pl.loop(0, half_tiles)
        def _(k):
            c_recv[k] = jnp.zeros((STATE, TILE), BF16)

    @pl.when(me > 0)
    def _():
        halo_copy.wait_recv()

    arrived = halo_recv[...].astype(F32) * survive
    for q in range(4):
        halo[8 - RIM :, q * quarter : (q + 1) * quarter] = arrived[RIM * q : RIM * q + RIM, :]

    kqs[:8, :] = halo[:, features:]
    kqs[8:, :] = kq_ref[...].astype(F32)
    wkq = wkq_ref[...].astype(F32)
    for i in range(2 * GRP_DEV):
        cs = slice(i * STATE, (i + 1) * STATE)
        acc = jnp.broadcast_to(bkq_ref[:, cs].astype(F32), (SPAN, STATE))
        for tap in range(KERNEL):
            acc = acc + wkq[tap : tap + 1, cs] * kqs[8 - RIM + tap : 8 - RIM + tap + SPAN, cs]
        act = silu(acc)
        if i < GRP_DEV:
            keys_t[i] = jnp.transpose(act).astype(BF16)
        else:
            queries[i - GRP_DEV] = act.astype(BF16)

    def span_state(t, g):
        cs = pl.ds(pl.multiple_of(t * TILE, TILE), TILE)
        xs[:8, :] = halo[:, cs]
        xs[8:, :] = x_ref[:, cs].astype(F32)
        wx = wx_ref[:, cs].astype(F32)
        acc = jnp.broadcast_to(bx_ref[:, cs].astype(F32), (SPAN, TILE))
        for tap in range(KERNEL):
            acc = acc + wx[tap : tap + 1] * xs[8 - RIM + tap : 8 - RIM + tap + SPAN, :]
        v = silu(acc).astype(BF16)
        vals[:, cs] = v
        weighted = (dot(w2[...], hot[:, cs]) * v.astype(F32)).astype(BF16)
        return dot(keys_t[g], weighted)

    other = 1 - side

    def s_copy(k):
        return remote(s_send.at[k], s_recv.at[k], s_ssem.at[k], s_rsem.at[k], partner)

    def c_copy(k):
        return remote(c_send.at[k], c_recv.at[k], c_ssem.at[k], c_rsem.at[k], jnp.minimum(me + 2, peers - 2 + side))

    def e_copy(k):
        return remote(e_send.at[k], e_recv.at[k], e_ssem.at[k], e_rsem.at[k], partner)

    @pl.loop(0, half_tiles)
    def _(k):
        s_send[k] = span_state(other * half_tiles + k, other).astype(BF16)
        s_copy(k).start()

    @pl.loop(0, half_tiles)
    def _(k):
        s_own[k] = span_state(side * half_tiles + k, side)

    for g in range(GRP_DEV):
        scores[g] = dot(queries[g], keys_t[g])

    f_copy.wait_recv()
    rows = jnp.concatenate(
        [factor, f_recv[:1, :], jnp.concatenate([skip, skip], axis=1), jnp.zeros((13, 2 * HEAD_DEV), F32)], axis=0
    )
    rows2[...] = two_terms(rows)
    ssq[...] = jnp.zeros_like(ssq)

    def local_part(t, g, skip_row):
        cs = pl.ds(pl.multiple_of(t * TILE, TILE), TILE)
        rolled = pltpu.roll(cum2[...], HEAD_DEV - t * TILE_HEADS, 1)
        sc = scores[g]
        cut = mask[...]
        lane = lax.broadcasted_iota(jnp.int32, (SPAN, 2 * HEAD_SIZE), 1)
        v_all = vals[:, cs]
        parts = []
        for pair in range(TILE_HEADS // 2):
            mixes = []
            for i in range(2):
                n = 2 * pair + i
                gap = rolled[:, n : n + 1] - row_t[pl.ds(t * TILE_HEADS + n, 1), :] + cut
                mixes.append((sc * jnp.exp2(gap)).astype(BF16))
            v = v_all[:, pair * 2 * HEAD_SIZE : (pair + 1) * 2 * HEAD_SIZE]
            vf = v.astype(F32)
            block = jnp.concatenate(
                [jnp.where(lane < HEAD_SIZE, vf, 0.0), jnp.where(lane < HEAD_SIZE, 0.0, vf)], axis=0
            ).astype(BF16)
            parts.append(dot(jnp.concatenate(mixes, axis=1), block))
        inside = jnp.concatenate(parts, axis=1)
        gate = silu(gate_ref[:, cs].astype(F32))
        res[:, cs] = (inside + skip_row * v_all.astype(F32)) * gate
        mix_gate[:, cs] = dot(g2[...], hot[:, cs]) * gate

    def read_back(t, g, entering):
        cs = pl.ds(pl.multiple_of(t * TILE, TILE), TILE)
        gated = res[:, cs] + mix_gate[:, cs] * dot(queries[g], entering)
        res[:, cs] = gated
        sq = gated * gated
        ssq[g] += sq[:, :STATE] + sq[:, STATE:]

    def finish(g):
        mean = jnp.sum(ssq[g], axis=1, keepdims=True) * (1.0 / (half_tiles * TILE))
        scale = lax.rsqrt(mean + 1e-05)

        @pl.loop(0, half_tiles)
        def _(k):
            cs = pl.ds(pl.multiple_of((g * half_tiles + k) * TILE, TILE), TILE)
            out_ref[:, cs] = ((res[:, cs] * scale) * gain_ref[:, cs]).astype(BF16)

    @pl.loop(0, half_tiles)
    def _(k):
        t = side * half_tiles + k
        u = other * half_tiles + k
        cs = pl.ds(pl.multiple_of(t * TILE, TILE), TILE)
        us = pl.ds(pl.multiple_of(u * TILE, TILE), TILE)
        own_rows = dot(rows2[...], hot[:, cs])
        other_rows = dot(rows2[...], hot[:, us])
        f_own = own_rows[0:1]
        f_oth = own_rows[1:2]
        s_copy(k).wait_recv()

        @pl.when(row > 0)
        def _():
            c_copy(k).wait_recv()

        @pl.when(side == 0)
        def _():
            mid = f_own * c_recv[k].astype(F32) + s_own[k]
            c_send[k] = (f_oth * mid + s_recv[k].astype(F32)).astype(BF16)
            e_send[k] = mid.astype(BF16)
            e_own[k] = c_recv[k]

        @pl.when(side == 1)
        def _():
            mid = f_oth * c_recv[k].astype(F32) + s_recv[k].astype(F32)
            c_send[k] = (f_own * mid + s_own[k]).astype(BF16)
            e_send[k] = c_recv[k]
            e_own[k] = mid.astype(BF16)

        @pl.when(row < last_row)
        def _():
            c_copy(k).start()

        e_copy(k).start()
        local_part(t, side, own_rows[2:3])
        read_back(t, side, e_own[k])
        local_part(u, other, other_rows[2:3])

    finish(side)

    @pl.loop(0, half_tiles)
    def _(k):
        e_copy(k).wait_recv()
        read_back(other * half_tiles + k, other, e_recv[k])

    finish(other)

    @pl.when(me < peers - 1)
    def _():
        halo_copy.wait_send()

    f_copy.wait_send()

    @pl.loop(0, half_tiles)
    def _(k):
        s_copy(k).wait_send()
        e_copy(k).wait_send()

        @pl.when(row < last_row)
        def _():
            c_copy(k).wait_send()


def shards(
    mixer_input,
    keys_queries,
    gate_input,
    step_raw,
    mixer_weight,
    mixer_bias,
    keyquery_weight,
    keyquery_bias,
    step_bias,
    decay_log,
    skip_gain,
    norm_gain,
    resets,
):
    length, features = mixer_input.shape
    peers = lax.axis_size("seq")
    pair_width = 2 * keys_queries.shape[2]
    tiles = features // TILE
    half = tiles // 2
    split = (features + pair_width) // 4
    vmem = pl.BlockSpec(memory_space=pltpu.VMEM)
    dma = pltpu.SemaphoreType.DMA
    chunk = (half, STATE, TILE)
    return pl.pallas_call(
        functools.partial(kernel, peers, tiles, split),
        out_shape=jax.ShapeDtypeStruct((length, features), BF16),
        in_specs=[vmem] * 12 + [pl.BlockSpec(memory_space=pltpu.SMEM)],
        out_specs=vmem,
        scratch_shapes=[
            pltpu.VMEM((16, split), BF16),
            pltpu.VMEM((16, split), BF16),
            pltpu.VMEM((8, features + pair_width), F32),
            pltpu.VMEM((SPAN + 8, TILE), F32),
            pltpu.VMEM((SPAN + 8, pair_width), F32),
            pltpu.VMEM((SPAN, features), BF16),
            pltpu.VMEM((SPAN, features), BF16),
            pltpu.VMEM((SPAN, 2 * HEAD_DEV), BF16),
            pltpu.VMEM((SPAN, 2 * HEAD_DEV), BF16),
            pltpu.VMEM((SPAN, 2 * HEAD_DEV), F32),
            pltpu.VMEM((2 * HEAD_DEV, SPAN), F32),
            pltpu.VMEM((GRP_DEV, STATE, SPAN), BF16),
            pltpu.VMEM((GRP_DEV, SPAN, STATE), BF16),
            pltpu.VMEM((GRP_DEV, SPAN, SPAN), F32),
            pltpu.VMEM((SPAN, SPAN), F32),
            pltpu.VMEM((16, 2 * HEAD_DEV), BF16),
            pltpu.VMEM((8, 2 * HEAD_DEV), F32),
            pltpu.VMEM((8, 2 * HEAD_DEV), F32),
            pltpu.VMEM(chunk, BF16),
            pltpu.VMEM(chunk, BF16),
            pltpu.VMEM(chunk, F32),
            pltpu.VMEM(chunk, BF16),
            pltpu.VMEM(chunk, BF16),
            pltpu.VMEM(chunk, BF16),
            pltpu.VMEM(chunk, BF16),
            pltpu.VMEM(chunk, BF16),
            pltpu.VMEM((SPAN, features), F32),
            pltpu.VMEM((SPAN, features), F32),
            pltpu.VMEM((GRP_DEV, SPAN, STATE), F32),
            dma((2,)),
            dma((2,)),
            dma((half,)),
            dma((half,)),
            dma((half,)),
            dma((half,)),
            dma((half,)),
            dma((half,)),
        ],
        compiler_params=pltpu.CompilerParams(
            collective_id=0, has_side_effects=True, vmem_limit_bytes=40 * 1024 * 1024
        ),
    )(
        mixer_input,
        keys_queries.reshape(length, pair_width),
        gate_input,
        step_raw,
        mixer_weight,
        mixer_bias.reshape(1, features),
        keyquery_weight.reshape(KERNEL, pair_width),
        keyquery_bias.reshape(1, pair_width),
        step_bias.reshape(1, HEAD_DEV),
        decay_log.reshape(1, HEAD_DEV),
        skip_gain.reshape(1, HEAD_DEV),
        norm_gain.reshape(1, features),
        resets,
    )


def solution(mesh):
    in_specs = (
        P(("groups", "seq"), "head"),
        P(("groups", "seq"), None, "head"),
        P(("groups", "seq"), "head"),
        P(("groups", "seq"), "head"),
        P(None, "head"),
        P("head"),
        P(None, None, "head"),
        P(None, "head"),
        P("head"),
        P("head"),
        P("head"),
        P("head"),
        P(("groups", "seq")),
    )
    out_specs = P(("groups", "seq"), "head")
    return jax.shard_map(shards, mesh=mesh, in_specs=in_specs, out_specs=out_specs, check_vma=False)
```

time: 323 us -> 39.4 us (0.12)
  the two profiles are of different devices: /device:TPU:0 before, /device:TPU:24 now
where the time goes in v1:
time: 39.4 us; the launch traced here: 39.1 us
  Pallas kernels  31.8 us (81%)
  local copies, waits for them, and re-layouts  6.52 us (17%)
  between operations  0.76 us (2%)
    pallas_call x1, Pallas kernels, shards(): pl.pallas_call(functools.partial(kernel, peers, tiles, split), out_shape=...  31.8 us
    unnamed x27, local copies, waits for them, and re-layouts  6.51 us

profile of v1, /device:TPU:24, one launch (start us, length us, event | category | flops | bytes accessed | tf_op | source)
XLA Modules:
  0.0 39.1 jit_solution(5364766535618464457)
XLA Ops:
  0.7 0.0 copy-start.10
  0.7 0.0 copy-start.9
  0.7 0.0 copy-start.8
  0.7 0.7 %copy-done.10 = bf16[2,256]{1,0:T(2,128)(2,1)S(1)} copy-done((bf16[2,256]{1,0:T(2,128)(2,1)S(1)}, bf16[2,256]{1,0:T(2,128)(2,1)}, u32[]{:S(2)}) %copy-start.10) | copy-done | bytes 1048
  1.3 0.0 copy-done.9
  1.4 0.0 copy-start.7
  1.4 0.0 copy-done.8
  1.4 0.7 %copy-done.7 = bf16[128,64]{0,1:T(8,128)(2,1)S(1)} copy-done((bf16[128,64]{0,1:T(8,128)(2,1)S(1)}, bf16[128,64]{0,1:T(8,128)(2,1)}, u32[]{:S(2)}) %copy-start.7) | copy-done | bytes 16408
  2.1 0.1 copy.14.step_ref
  2.2 0.0 copy-start.2
  2.2 0.0 copy-start.3
  2.2 0.9 %copy.15 = bf16[16,8,2,256]{3,1,2,0:T(8,128)(2,1)S(1)} copy(bf16[16,8,2,256]{3,2,1,0:T(2,128)(2,1)} %bitcast.18) | data formatting | bytes 262144
  3.2 0.0 copy-start.4
  3.2 0.0 copy-start.5
  3.2 0.0 copy-start.6
  3.2 0.0 copy-done.2
  3.2 0.0 copy-done.3
  3.2 0.6 %copy-done.4 = f32[64]{0:T(128)S(1)} copy-done((f32[64]{0:T(128)S(1)}, f32[64]{0:T(128)}, u32[]{:S(2)}) %copy-start.4) | copy-done | bytes 280
  3.8 0.0 copy-done.5
  3.8 0.0 copy-done.6
  3.8 0.0 copy-start
  3.8 1.2 %copy-done = bf16[128,4096]{1,0:T(8,128)(2,1)S(1)} copy-done((bf16[128,4096]{1,0:T(8,128)(2,1)S(1)}, bf16[128,4096]{1,0:T(8,128)(2,1)}, u32[]{:S(2)}) %copy-start) | copy-done | bytes 1048600
  5.1 0.0 copy-start.1
  5.1 1.2 %copy-done.1 = bf16[128,4096]{1,0:T(8,128)(2,1)S(1)} copy-done((bf16[128,4096]{1,0:T(8,128)(2,1)S(1)}, bf16[128,4096]{1,0:T(8,128)(2,1)}, u32[]{:S(2)}) %copy-start.1) | copy-done | bytes 1048600
  6.3 31.8 %shard_map.127 = bf16[128,4096]{1,0:T(8,128)(2,1)S(1)} custom-call(bf16[128,4096]{1,0:T(8,128)(2,1)S(1)} %copy-done, bf16[128,512]{1,0:T(8,128)(2,1)S(1)} %bitcast.11, bf16[128,4096]{1,0:T(8,128)(2,1)S(1)} %copy-done.1, bf16[128,64]{1,0:T(8,128)(2,1)S(1)} %copy.14.step_ref, bf16[4,4096]{1,0:T(4,128)(2,1)S(1)} %copy-done.2, ...), custom_call_target="tpu_custom_call" | custom-call | tf_op jit(solution)/shard_map/pallas_call | solution.py:318
  38.1 1.0 %copy.20 = bf16[128,4096]{1,0:T(8,128)(2,1)} copy(bf16[128,4096]{1,0:T(8,128)(2,1)S(1)} %shard_map.127) | data formatting | bytes 2097152
  (3 shorter events, 0.0 us)
Async XLA Ops:
  0.7 0.7 %copy-start.10 = (bf16[2,256]{1,0:T(2,128)(2,1)S(1)}, bf16[2,256]{1,0:T(2,128)(2,1)}, u32[]{:S(2)}) copy-start(bf16[2,256]{1,0:T(2,128)(2,1)} %param.20) | copy-start | bytes 3076
  0.7 0.7 %copy-start.9 = (bf16[4,2,256]{2,1,0:T(2,128)(2,1)S(1)}, bf16[4,2,256]{2,1,0:T(2,128)(2,1)}, u32[]{:S(2)}) copy-start(bf16[4,2,256]{2,1,0:T(2,128)(2,1)} %param.19) | copy-start | bytes 12292
  0.7 0.7 %copy-start.8 = (bf16[4096]{0:T(1024)(128)(2,1)S(1)}, bf16[4096]{0:T(1024)(128)(2,1)}, u32[]{:S(2)}) copy-start(bf16[4096]{0:T(1024)(128)(2,1)} %param.18) | copy-start | bytes 24580
  1.4 0.7 %copy-start.7 = (bf16[128,64]{0,1:T(8,128)(2,1)S(1)}, bf16[128,64]{0,1:T(8,128)(2,1)}, u32[]{:S(2)}) copy-start(bf16[128,64]{0,1:T(8,128)(2,1)} %param.16) | copy-start | bytes 49156
  2.2 1.0 %copy-start.2 = (bf16[4,4096]{1,0:T(4,128)(2,1)S(1)}, bf16[4,4096]{1,0:T(4,128)(2,1)}, u32[]{:S(2)}) copy-start(bf16[4,4096]{1,0:T(4,128)(2,1)} %wx_ref.1) | copy-start | bytes 98308
  2.2 1.0 %copy-start.3 = (f32[4096]{0:T(1024)S(1)}, f32[4096]{0:T(1024)}, u32[]{:S(2)}) copy-start(f32[4096]{0:T(1024)} %param.24) | copy-start | bytes 49156
  3.2 0.7 %copy-start.4 = (f32[64]{0:T(128)S(1)}, f32[64]{0:T(128)}, u32[]{:S(2)}) copy-start(f32[64]{0:T(128)} %param.21) | copy-start | bytes 772
  3.2 0.7 %copy-start.5 = (f32[64]{0:T(128)S(1)}, f32[64]{0:T(128)}, u32[]{:S(2)}) copy-start(f32[64]{0:T(128)} %param.22) | copy-start | bytes 772
  3.2 0.7 %copy-start.6 = (f32[64]{0:T(128)S(1)}, f32[64]{0:T(128)}, u32[]{:S(2)}) copy-start(f32[64]{0:T(128)} %param.23) | copy-start | bytes 772
  3.8 1.2 %copy-start = (bf16[128,4096]{1,0:T(8,128)(2,1)S(1)}, bf16[128,4096]{1,0:T(8,128)(2,1)}, u32[]{:S(2)}) copy-start(bf16[128,4096]{1,0:T(8,128)(2,1)} %x_ref.1) | copy-start | bytes 3145732
  5.1 1.2 %copy-start.1 = (bf16[128,4096]{1,0:T(8,128)(2,1)S(1)}, bf16[128,4096]{1,0:T(8,128)(2,1)}, u32[]{:S(2)}) copy-start(bf16[128,4096]{1,0:T(8,128)(2,1)} %gate_ref.1) | copy-start | bytes 3145732

commit v2 on v1

--- a/solution.py
+++ b/solution.py
@@ -39,9 +39,11 @@
 
 def kernel(
     peers, tiles, split,
-    x_ref, kq_ref, gate_ref, step_ref, wx_ref, bx_ref, wkq_ref, bkq_ref,
-    sbias_ref, dlog_ref, skip_ref, gain_ref, resets_ref,
+    x_hbm, kq_hbm, gate_hbm, step_hbm, wx_hbm, bx_hbm, wkq_hbm, bkq_hbm,
+    sbias_hbm, dlog_hbm, skip_hbm, gain_hbm, resets_ref,
     out_ref,
+    x_ref, kq_ref, gate_ref, step_ref, wx_ref, bx_ref, wkq_ref, bkq_ref, sbias_ref, dlog_ref, skip_ref, gain_ref,
+    tail_ref, in_sem, bx,
     halo_send, halo_recv, halo, xs, kqs, vals, hot, w2, g2, cum2, row_t, keys_t, queries, scores, mask,
     rows2, f_send, f_recv, s_send, s_recv, s_own, c_recv, c_send, e_send, e_recv, e_own, res, mix_gate, ssq,
     one_send, one_recv, s_ssem, s_rsem, c_ssem, c_rsem, e_ssem, e_rsem,
@@ -55,14 +57,24 @@
     half_tiles = tiles // 2
     quarter = split
 
+    sources = (x_hbm.at[SPAN - 16 :], kq_hbm, step_hbm, sbias_hbm, dlog_hbm, skip_hbm, wkq_hbm, bkq_hbm, x_hbm,
+               wx_hbm, bx_hbm, gate_hbm, gain_hbm)
+    places = (tail_ref, kq_ref, step_ref, sbias_ref, dlog_ref, skip_ref, wkq_ref, bkq_ref, x_ref,
+              wx_ref, bx_ref, gate_ref, gain_ref)
+    loads = [pltpu.make_async_copy(src, dst, in_sem.at[i]) for i, (src, dst) in enumerate(zip(sources, places))]
+    for load in loads:
+        load.start()
     barrier = pltpu.get_barrier_semaphore()
     for away in (-2, -1, 1, 2):
         @pl.when((me + away >= 0) & (me + away < peers))
         def _(away=away):
             pl.semaphore_signal(barrier, inc=1, device_id={"seq": me + away}, device_id_type=MESH)
-    rim = jnp.concatenate(
-        [x_ref[SPAN - 16 :, :].astype(F32)[16 - RIM :], kq_ref[SPAN - 16 :, :].astype(F32)[16 - RIM :]], axis=1
-    )
+    loads[0].wait()
+    loads[1].wait()
+    pairs = kq_ref[...].astype(F32)
+    pairs = jnp.concatenate([pairs[:, 0, :], pairs[:, 1, :]], axis=1)
+    kqs[8:, :] = pairs
+    rim = jnp.concatenate([tail_ref[...].astype(F32)[16 - RIM :], pairs[SPAN - RIM :]], axis=1)
     rim_parts = [rim[:, q * quarter : (q + 1) * quarter] for q in range(4)]
     halo_send[...] = jnp.concatenate(rim_parts + [jnp.zeros((4, quarter), F32)], axis=0).astype(BF16)
     pl.semaphore_wait(barrier, jnp.minimum(me, 2) + jnp.minimum(peers - 1 - me, 2))
@@ -84,8 +96,10 @@
 
     survive = 1.0 - resets_ref[0].astype(F32)
 
+    for load in loads[2:6]:
+        load.wait()
     raw = step_ref[...].astype(F32)
-    both = jnp.concatenate([raw, raw], axis=1)
+    both = jnp.transpose(jnp.concatenate([raw, raw], axis=0))
     sbias = sbias_ref[...]
     dlog = dlog_ref[...]
     skip = skip_ref[...]
@@ -130,11 +144,16 @@
         halo[8 - RIM :, q * quarter : (q + 1) * quarter] = arrived[RIM * q : RIM * q + RIM, :]
 
     kqs[:8, :] = halo[:, features:]
-    kqs[8:, :] = kq_ref[...].astype(F32)
+    for load in loads[6:11]:
+        load.wait()
     wkq = wkq_ref[...].astype(F32)
+    wkq = jnp.concatenate([wkq[:, 0, :], wkq[:, 1, :]], axis=1)
+    bkq = bkq_ref[...].astype(F32)
+    bkq = jnp.concatenate([bkq[:1], bkq[1:]], axis=1)
+    bx[...] = bx_ref[...].astype(F32).reshape(1, features)
     for i in range(2 * GRP_DEV):
         cs = slice(i * STATE, (i + 1) * STATE)
-        acc = jnp.broadcast_to(bkq_ref[:, cs].astype(F32), (SPAN, STATE))
+        acc = jnp.broadcast_to(bkq[:, cs], (SPAN, STATE))
         for tap in range(KERNEL):
             acc = acc + wkq[tap : tap + 1, cs] * kqs[8 - RIM + tap : 8 - RIM + tap + SPAN, cs]
         act = silu(acc)
@@ -148,7 +167,7 @@
         xs[:8, :] = halo[:, cs]
         xs[8:, :] = x_ref[:, cs].astype(F32)
         wx = wx_ref[:, cs].astype(F32)
-        acc = jnp.broadcast_to(bx_ref[:, cs].astype(F32), (SPAN, TILE))
+        acc = jnp.broadcast_to(bx[:, cs], (SPAN, TILE))
         for tap in range(KERNEL):
             acc = acc + wx[tap : tap + 1] * xs[8 - RIM + tap : 8 - RIM + tap + SPAN, :]
         v = silu(acc).astype(BF16)
@@ -176,6 +195,8 @@
     def _(k):
         s_own[k] = span_state(side * half_tiles + k, side)
 
+    loads[11].wait()
+    loads[12].wait()
     for g in range(GRP_DEV):
         scores[g] = dot(queries[g], keys_t[g])
 
@@ -313,14 +334,33 @@
     half = tiles // 2
     split = (features + pair_width) // 4
     vmem = pl.BlockSpec(memory_space=pltpu.VMEM)
+    hbm = pl.BlockSpec(memory_space=pltpu.HBM)
+    operands = (
+        mixer_input,
+        keys_queries,
+        gate_input,
+        step_raw.T,
+        mixer_weight,
+        mixer_bias,
+        keyquery_weight,
+        keyquery_bias,
+        step_bias.reshape(1, HEAD_DEV),
+        decay_log.reshape(1, HEAD_DEV),
+        skip_gain.reshape(1, HEAD_DEV),
+        norm_gain.reshape(1, features),
+    )
     dma = pltpu.SemaphoreType.DMA
     chunk = (half, STATE, TILE)
     return pl.pallas_call(
         functools.partial(kernel, peers, tiles, split),
         out_shape=jax.ShapeDtypeStruct((length, features), BF16),
-        in_specs=[vmem] * 12 + [pl.BlockSpec(memory_space=pltpu.SMEM)],
+        in_specs=[hbm] * 12 + [pl.BlockSpec(memory_space=pltpu.SMEM)],
         out_specs=vmem,
-        scratch_shapes=[
+        scratch_shapes=[pltpu.VMEM(a.shape, a.dtype) for a in operands]
+        + [
+            pltpu.VMEM((16, features), BF16),
+            dma((13,)),
+            pltpu.VMEM((1, features), F32),
             pltpu.VMEM((16, split), BF16),
             pltpu.VMEM((16, split), BF16),
             pltpu.VMEM((8, features + pair_width), F32),
@@ -360,23 +400,9 @@
             dma((half,)),
         ],
         compiler_params=pltpu.CompilerParams(
-            collective_id=0, has_side_effects=True, vmem_limit_bytes=40 * 1024 * 1024
+            collective_id=0, has_side_effects=True, vmem_limit_bytes=60 * 1024 * 1024
         ),
-    )(
-        mixer_input,
-        keys_queries.reshape(length, pair_width),
-        gate_input,
-        step_raw,
-        mixer_weight,
-        mixer_bias.reshape(1, features),
-        keyquery_weight.reshape(KERNEL, pair_width),
-        keyquery_bias.reshape(1, pair_width),
-        step_bias.reshape(1, HEAD_DEV),
-        decay_log.reshape(1, HEAD_DEV),
-        skip_gain.reshape(1, HEAD_DEV),
-        norm_gain.reshape(1, features),
-        resets,
-    )
+    )(*operands, resets)
 
 
 def solution(mesh):

time: 39.4 us -> 36.4 us (0.924)
  local copies, waits for them, and re-layouts: 6.52 us -> 2.29 us
  Pallas kernels: 31.8 us -> 33.2 us
    unnamed x27 -> x1, local copies, waits for them, and re-layouts: 6.51 us -> 2.29 us
    pallas_call x1, Pallas kernels: 31.8 us -> 33.2 us  [shards(): pl.pallas_call(functools.partial(kernel, peers, tiles, split), out_shape=...]
where the time goes in v2:
time: 36.4 us; the launch traced here: 36.2 us
  Pallas kernels  33.2 us (91%)
  local copies, waits for them, and re-layouts  2.29 us (6%)
  between operations  0.66 us (2%)
    pallas_call x1, Pallas kernels, shards(): pl.pallas_call(functools.partial(kernel, peers, tiles, split), out_shape=...  33.2 us
    unnamed x1, local copies, waits for them, and re-layouts  2.29 us

profile of v2, /device:TPU:24, one launch (start us, length us, event | category | flops | bytes accessed | tf_op | source)
XLA Modules:
  0.0 36.2 jit_solution(10227094608080006337)
XLA Ops:
  0.7 33.2 %shard_map.127 = bf16[128,4096]{1,0:T(8,128)(2,1)} custom-call(bf16[128,4096]{1,0:T(8,128)(2,1)} %x_hbm.1, bf16[128,2,256]{2,1,0:T(2,128)(2,1)} %kq_hbm.1, bf16[128,4096]{1,0:T(8,128)(2,1)} %gate_hbm.1, bf16[64,128]{1,0:T(8,128)(2,1)} %bitcast.5, bf16[4,4096]{1,0:T(4,128)(2,1)} %wx_hbm.1, bf16[4096]{0:T(1024)(128)(2,1)} %bx_hbm.1, ...), custom_call_target="tpu_custom_call" | custom-call | tf_op jit(solution)/shard_map/pallas_call | solution.py:354
  33.9 2.3 %copy.16 = bf16[128,4096]{1,0:T(8,128)(2,1)} copy(bf16[128,4096]{1,0:T(8,128)(2,1)} %shard_map.127) | data formatting | bytes 2097152

commit v3 on v2

--- a/solution.py
+++ b/solution.py
@@ -40,10 +40,10 @@
 def kernel(
     peers, tiles, split,
     x_hbm, kq_hbm, gate_hbm, step_hbm, wx_hbm, bx_hbm, wkq_hbm, bkq_hbm,
-    sbias_hbm, dlog_hbm, skip_hbm, gain_hbm, resets_ref,
+    sbias_hbm, dlog_hbm, skip_hbm, resets_ref,
     out_ref,
-    x_ref, kq_ref, gate_ref, step_ref, wx_ref, bx_ref, wkq_ref, bkq_ref, sbias_ref, dlog_ref, skip_ref, gain_ref,
-    tail_ref, in_sem, bx,
+    x_ref, kq_ref, gate_ref, step_ref, wx_ref, bx_ref, wkq_ref, bkq_ref, sbias_ref, dlog_ref, skip_ref,
+    tail_ref, in_sem, bx, out_sem,
     halo_send, halo_recv, halo, xs, kqs, vals, hot, w2, g2, cum2, row_t, keys_t, queries, scores, mask,
     rows2, f_send, f_recv, s_send, s_recv, s_own, c_recv, c_send, e_send, e_recv, e_own, res, mix_gate, ssq,
     one_send, one_recv, s_ssem, s_rsem, c_ssem, c_rsem, e_ssem, e_rsem,
@@ -58,9 +58,9 @@
     quarter = split
 
     sources = (x_hbm.at[SPAN - 16 :], kq_hbm, step_hbm, sbias_hbm, dlog_hbm, skip_hbm, wkq_hbm, bkq_hbm, x_hbm,
-               wx_hbm, bx_hbm, gate_hbm, gain_hbm)
+               wx_hbm, bx_hbm, gate_hbm)
     places = (tail_ref, kq_ref, step_ref, sbias_ref, dlog_ref, skip_ref, wkq_ref, bkq_ref, x_ref,
-              wx_ref, bx_ref, gate_ref, gain_ref)
+              wx_ref, bx_ref, gate_ref)
     loads = [pltpu.make_async_copy(src, dst, in_sem.at[i]) for i, (src, dst) in enumerate(zip(sources, places))]
     for load in loads:
         load.start()
@@ -69,6 +69,14 @@
         @pl.when((me + away >= 0) & (me + away < peers))
         def _(away=away):
             pl.semaphore_signal(barrier, inc=1, device_id={"seq": me + away}, device_id_type=MESH)
+    @pl.loop(0, tiles)
+    def _(t):
+        r = lax.broadcasted_iota(jnp.int32, (SPAN, TILE), 0)
+        c = lax.broadcasted_iota(jnp.int32, (SPAN, TILE), 1)
+        hot[:, pl.ds(pl.multiple_of(t * TILE, TILE), TILE)] = (
+            ((r & (HEAD_DEV - 1)) == t * TILE_HEADS + (c >> 6)).astype(F32).astype(BF16)
+        )
+
     loads[0].wait()
     loads[1].wait()
     pairs = kq_ref[...].astype(F32)
@@ -121,20 +129,6 @@
     row_t[...] = jnp.transpose(cum - jnp.log2(step))
     mask[...] = jnp.where(t_idx >= s_idx, 0.0, -1e30)
 
-    @pl.loop(0, tiles)
-    def _(t):
-        r = lax.broadcasted_iota(jnp.int32, (SPAN, TILE), 0)
-        c = lax.broadcasted_iota(jnp.int32, (SPAN, TILE), 1)
-        hot[:, pl.ds(pl.multiple_of(t * TILE, TILE), TILE)] = (
-            ((r & (HEAD_DEV - 1)) == t * TILE_HEADS + (c >> 6)).astype(F32).astype(BF16)
-        )
-
-    @pl.when(row == 0)
-    def _():
-        @pl.loop(0, half_tiles)
-        def _(k):
-            c_recv[k] = jnp.zeros((STATE, TILE), BF16)
-
     @pl.when(me > 0)
     def _():
         halo_copy.wait_recv()
@@ -196,7 +190,12 @@
         s_own[k] = span_state(side * half_tiles + k, side)
 
     loads[11].wait()
-    loads[12].wait()
+    @pl.when(row == 0)
+    def _():
+        @pl.loop(0, half_tiles)
+        def _(k):
+            c_recv[k] = jnp.zeros((STATE, TILE), BF16)
+
     for g in range(GRP_DEV):
         scores[g] = dot(queries[g], keys_t[g])
 
@@ -239,6 +238,10 @@
         sq = gated * gated
         ssq[g] += sq[:, :STATE] + sq[:, STATE:]
 
+    def out_copy(g, k):
+        cs = pl.ds(pl.multiple_of((g * half_tiles + k) * TILE, TILE), TILE)
+        return pltpu.make_async_copy(res.at[:, cs], out_ref.at[:, cs], out_sem.at[g, k])
+
     def finish(g):
         mean = jnp.sum(ssq[g], axis=1, keepdims=True) * (1.0 / (half_tiles * TILE))
         scale = lax.rsqrt(mean + 1e-05)
@@ -246,16 +249,21 @@
         @pl.loop(0, half_tiles)
         def _(k):
             cs = pl.ds(pl.multiple_of((g * half_tiles + k) * TILE, TILE), TILE)
-            out_ref[:, cs] = ((res[:, cs] * scale) * gain_ref[:, cs]).astype(BF16)
-
-    @pl.loop(0, half_tiles)
-    def _(k):
+            res[:, cs] = res[:, cs] * scale
+            out_copy(g, k).start()
+
+    def local_step(k):
         t = side * half_tiles + k
         u = other * half_tiles + k
+        skips = [dot(rows2[...], hot[:, pl.ds(pl.multiple_of(n * TILE, TILE), TILE)])[2:3] for n in (t, u)]
+        local_part(t, side, skips[0])
+        local_part(u, other, skips[1])
+
+    @pl.loop(0, half_tiles)
+    def _(k):
+        t = side * half_tiles + k
         cs = pl.ds(pl.multiple_of(t * TILE, TILE), TILE)
-        us = pl.ds(pl.multiple_of(u * TILE, TILE), TILE)
         own_rows = dot(rows2[...], hot[:, cs])
-        other_rows = dot(rows2[...], hot[:, us])
         f_own = own_rows[0:1]
         f_oth = own_rows[1:2]
         s_copy(k).wait_recv()
@@ -283,9 +291,8 @@
             c_copy(k).start()
 
         e_copy(k).start()
-        local_part(t, side, own_rows[2:3])
+        local_step(k)
         read_back(t, side, e_own[k])
-        local_part(u, other, other_rows[2:3])
 
     finish(side)
 
@@ -295,6 +302,11 @@
         read_back(other * half_tiles + k, other, e_recv[k])
 
     finish(other)
+
+    @pl.loop(0, half_tiles)
+    def _(k):
+        out_copy(side, k).wait()
+        out_copy(other, k).wait()
 
     @pl.when(me < peers - 1)
     def _():
@@ -333,7 +345,6 @@
     tiles = features // TILE
     half = tiles // 2
     split = (features + pair_width) // 4
-    vmem = pl.BlockSpec(memory_space=pltpu.VMEM)
     hbm = pl.BlockSpec(memory_space=pltpu.HBM)
     operands = (
         mixer_input,
@@ -347,20 +358,20 @@
         step_bias.reshape(1, HEAD_DEV),
         decay_log.reshape(1, HEAD_DEV),
         skip_gain.reshape(1, HEAD_DEV),
-        norm_gain.reshape(1, features),
     )
     dma = pltpu.SemaphoreType.DMA
     chunk = (half, STATE, TILE)
-    return pl.pallas_call(
+    normed = pl.pallas_call(
         functools.partial(kernel, peers, tiles, split),
-        out_shape=jax.ShapeDtypeStruct((length, features), BF16),
-        in_specs=[hbm] * 12 + [pl.BlockSpec(memory_space=pltpu.SMEM)],
-        out_specs=vmem,
+        out_shape=jax.ShapeDtypeStruct((length, features), F32),
+        in_specs=[hbm] * 11 + [pl.BlockSpec(memory_space=pltpu.SMEM)],
+        out_specs=hbm,
         scratch_shapes=[pltpu.VMEM(a.shape, a.dtype) for a in operands]
         + [
             pltpu.VMEM((16, features), BF16),
-            dma((13,)),
+            dma((12,)),
             pltpu.VMEM((1, features), F32),
+            dma((2, half)),
             pltpu.VMEM((16, split), BF16),
             pltpu.VMEM((16, split), BF16),
             pltpu.VMEM((8, features + pair_width), F32),
@@ -403,6 +414,7 @@
             collective_id=0, has_side_effects=True, vmem_limit_bytes=60 * 1024 * 1024
         ),
     )(*operands, resets)
+    return (normed * norm_gain).astype(BF16)
 
 
 def solution(mesh):

time: 36.4 us -> 37.1 us (1.019)
  other arithmetic: 0 us -> 2.73 us
  local copies, waits for them, and re-layouts: 2.29 us -> 0.01 us
    convert_element_type x0 -> x1, other arithmetic: none -> 2.73 us  [shards(): return (normed * norm_gain).astype(BF16)]
    unnamed x1 -> x2, local copies, waits for them, and re-layouts: 2.29 us -> 0.01 us
where the time goes in v3:
time: 37.1 us; the launch traced here: 36.9 us
  Pallas kernels  33.5 us (90%)
  other arithmetic  2.73 us (7%)
  between operations  0.68 us (2%)
    pallas_call x1, Pallas kernels, shards(): pl.pallas_call(functools.partial(kernel, peers, tiles, split), out_shape=...  33.5 us
    convert_element_type x1, other arithmetic, shards(): return (normed * norm_gain).astype(BF16)  2.73 us

profile of v3, /device:TPU:24, one launch (start us, length us, event | category | flops | bytes accessed | tf_op | source)
XLA Modules:
  0.0 36.9 jit_solution(7485235447578859126)
XLA Ops:
  0.7 0.0 copy-start
  0.7 33.5 %shard_map.127 = f32[128,4096]{1,0:T(8,128)} custom-call(bf16[128,4096]{1,0:T(8,128)(2,1)} %x_hbm.1, bf16[128,2,256]{2,1,0:T(2,128)(2,1)} %kq_hbm.1, bf16[128,4096]{1,0:T(8,128)(2,1)} %gate_hbm.1, bf16[64,128]{1,0:T(8,128)(2,1)} %bitcast.4, bf16[4,4096]{1,0:T(4,128)(2,1)} %wx_hbm.1, bf16[4096]{0:T(1024)(128)(2,1)} %bx_hbm.1, bf16[4,2,256]{2,1,0:T(2,128)(2,1)} %wkq_hbm.1, ...), custom_call_target="tpu_custom_call" | custom-call | tf_op jit(solution)/shard_map/pallas_call | solution.py:364
  34.2 0.0 copy-done
  34.2 2.7 %multiply_convert_fusion = bf16[128,4096]{1,0:T(8,128)(2,1)} fusion(f32[128,4096]{1,0:T(8,128)} %shard_map.127, f32[4096]{0:T(1024)S(1)} %copy-done), kind=kLoop, calls=%fused_computation | loop fusion | flops 1048576 | bytes 3162112 | tf_op jit(solution)/shard_map/convert_element_type | solution.py:417
Async XLA Ops:
  0.7 33.5 %copy-start = (f32[4096]{0:T(1024)S(1)}, f32[4096]{0:T(1024)}, u32[]{:S(2)}) copy-start(f32[4096]{0:T(1024)} %param.24) | copy-start | bytes 49156

commit v4 on v2

--- a/solution.py
+++ b/solution.py
@@ -71,10 +71,9 @@
             pl.semaphore_signal(barrier, inc=1, device_id={"seq": me + away}, device_id_type=MESH)
     loads[0].wait()
     loads[1].wait()
-    pairs = kq_ref[...].astype(F32)
-    pairs = jnp.concatenate([pairs[:, 0, :], pairs[:, 1, :]], axis=1)
-    kqs[8:, :] = pairs
-    rim = jnp.concatenate([tail_ref[...].astype(F32)[16 - RIM :], pairs[SPAN - RIM :]], axis=1)
+    last = kq_ref[SPAN - 8 :].astype(F32)
+    last = jnp.concatenate([last[:, 0, :], last[:, 1, :]], axis=1)
+    rim = jnp.concatenate([tail_ref[...].astype(F32)[16 - RIM :], last[8 - RIM :]], axis=1)
     rim_parts = [rim[:, q * quarter : (q + 1) * quarter] for q in range(4)]
     halo_send[...] = jnp.concatenate(rim_parts + [jnp.zeros((4, quarter), F32)], axis=0).astype(BF16)
     pl.semaphore_wait(barrier, jnp.minimum(me, 2) + jnp.minimum(peers - 1 - me, 2))
@@ -95,6 +94,9 @@
         halo_recv[...] = jnp.zeros_like(halo_recv)
 
     survive = 1.0 - resets_ref[0].astype(F32)
+
+    pairs = kq_ref[...].astype(F32)
+    kqs[8:, :] = jnp.concatenate([pairs[:, 0, :], pairs[:, 1, :]], axis=1)
 
     for load in loads[2:6]:
         load.wait()

time: 36.4 us -> 36.5 us (level)
  no operation moved by 1% of the time
where the time goes in v4:
time: 36.5 us; the launch traced here: 36.3 us
  Pallas kernels  33.4 us (92%)
  local copies, waits for them, and re-layouts  2.29 us (6%)
  between operations  0.66 us (2%)
    pallas_call x1, Pallas kernels, shards(): pl.pallas_call(functools.partial(kernel, peers, tiles, split), out_shape=...  33.4 us
    unnamed x1, local copies, waits for them, and re-layouts  2.29 us

profile of v4, /device:TPU:24, one launch (start us, length us, event | category | flops | bytes accessed | tf_op | source)
XLA Modules:
  0.0 36.3 jit_solution(12254276059872940610)
XLA Ops:
  0.7 33.4 %shard_map.127 = bf16[128,4096]{1,0:T(8,128)(2,1)} custom-call(bf16[128,4096]{1,0:T(8,128)(2,1)} %x_hbm.1, bf16[128,2,256]{2,1,0:T(2,128)(2,1)} %kq_hbm.1, bf16[128,4096]{1,0:T(8,128)(2,1)} %gate_hbm.1, bf16[64,128]{1,0:T(8,128)(2,1)} %bitcast.5, bf16[4,4096]{1,0:T(4,128)(2,1)} %wx_hbm.1, bf16[4096]{0:T(1024)(128)(2,1)} %bx_hbm.1, ...), custom_call_target="tpu_custom_call" | custom-call | tf_op jit(solution)/shard_map/pallas_call | solution.py:356
  34.0 2.3 %copy.16 = bf16[128,4096]{1,0:T(8,128)(2,1)} copy(bf16[128,4096]{1,0:T(8,128)(2,1)} %shard_map.127) | data formatting | bytes 2097152

commit v5 on v2

--- a/solution.py
+++ b/solution.py
@@ -287,9 +287,14 @@
         read_back(t, side, e_own[k])
         local_part(u, other, other_rows[2:3])
 
+        @pl.when((row == last_row) & (k >= 2))
+        def _():
+            e_copy(k - 2).wait_recv()
+            read_back(u - 2, other, e_recv[k - 2])
+
     finish(side)
 
-    @pl.loop(0, half_tiles)
+    @pl.loop((row // last_row) * (half_tiles - 2), half_tiles)
     def _(k):
         e_copy(k).wait_recv()
         read_back(other * half_tiles + k, other, e_recv[k])

time: 36.4 us -> 38 us (1.044)
  Pallas kernels: 33.2 us -> 34.9 us
    pallas_call x1, Pallas kernels: 33.2 us -> 34.9 us  [shards(): pl.pallas_call(functools.partial(kernel, peers, tiles, split), out_shape=...]
where the time goes in v5:
time: 38 us; the launch traced here: 37.8 us
  Pallas kernels  34.9 us (92%)
  local copies, waits for them, and re-layouts  2.29 us (6%)
  between operations  0.66 us (2%)
    pallas_call x1, Pallas kernels, shards(): pl.pallas_call(functools.partial(kernel, peers, tiles, split), out_shape=...  34.9 us
    unnamed x1, local copies, waits for them, and re-layouts  2.29 us

profile of v5, /device:TPU:24, one launch (start us, length us, event | category | flops | bytes accessed | tf_op | source)
XLA Modules:
  0.0 37.8 jit_solution(13891933499916328712)
XLA Ops:
  0.7 34.9 %shard_map.127 = bf16[128,4096]{1,0:T(8,128)(2,1)} custom-call(bf16[128,4096]{1,0:T(8,128)(2,1)} %x_hbm.1, bf16[128,2,256]{2,1,0:T(2,128)(2,1)} %kq_hbm.1, bf16[128,4096]{1,0:T(8,128)(2,1)} %gate_hbm.1, bf16[64,128]{1,0:T(8,128)(2,1)} %bitcast.5, bf16[4,4096]{1,0:T(4,128)(2,1)} %wx_hbm.1, bf16[4096]{0:T(1024)(128)(2,1)} %bx_hbm.1, ...), custom_call_target="tpu_custom_call" | custom-call | tf_op jit(solution)/shard_map/pallas_call | solution.py:359
  35.5 2.3 %copy.16 = bf16[128,4096]{1,0:T(8,128)(2,1)} copy(bf16[128,4096]{1,0:T(8,128)(2,1)} %shard_map.127) | data formatting | bytes 2097152
